TPU v7x, 32 devices: a whole 2x2x4 slice. The times are simulated.
32 devices in a mesh: row: 4 (over y, x), col: 4 (over z), dp: 2 (over core).
Axes of the slice: x: 2, y: 2, z: 4, core: 2. Of those that a mesh axis runs over, the one named last changes fastest.
Arguments:
- inputs: bfloat16 [1024, 8192], P(('col', 'dp'), 'row'), may hold values from -6 to 6
- gate_weight: bfloat16 [8192, 14336], P('row', 'col'), may hold values from -0.0625 to 0.0625
- up_weight: bfloat16 [8192, 14336], P('row', 'col'), may hold values from -0.0625 to 0.0625
- down_weight: bfloat16 [14336, 8192], P('col', 'row'), may hold values from -0.046875 to 0.046875
- reward_head: bfloat16 [8192], P('row'), may hold values from -0.0625 to 0.0625
- upstream: bfloat16 [1024, 8192], P(('col', 'dp'), 'row'), may hold values from -0.59765625 to 0.59765625
- labels: int32 [1024], P(('col', 'dp')), may hold values from 0 to 1
- label_mask: int32 [1024], P(('col', 'dp')), may hold values 0 or 1
Outputs:
- gate_grad: float32 [8192, 14336], P(('row', 'dp'), 'col')
- up_grad: float32 [8192, 14336], P(('row', 'dp'), 'col')
- down_grad: float32 [14336, 8192], P(('col', 'dp'), 'row')
- input_grad: float32 [1024, 8192], P(('col', 'dp'), 'row')
All inputs are finite; a program needn't handle non-finite values. No bound on the sum of `label_mask` on one device may be relied on, other than what follows from the above.
Results may differ from a plain program's by a relative error of at most 0.035.
Values may be sent and summed in bfloat16 or wider, within the bound.
A program may use at most 192 MiB of HBM per device.

v0:
```python
import jax
import jax.numpy as jnp
from jax import lax
from jax.sharding import PartitionSpec as P

reward_weight = 8.0


def transpose_product(left, right):
    return lax.dot_general(
        left, right, (((0,), (0,)), ((), ())), preferred_element_type=jnp.float32
    )


def right_transpose(left, right):
    return lax.dot_general(
        left, right, (((1,), (1,)), ((), ())), preferred_element_type=jnp.float32
    )


def gather_tokens(block):
    return lax.all_gather(block, "col", axis=0, tiled=True)


def gather_hidden(stacked):
    return lax.all_gather(stacked, "row", axis=1, tiled=True)


def column_total(term_fn, count_rows):
    return lax.psum_scatter(
        term_fn(jnp.int32(0), count_rows * lax.axis_size("col")).astype(jnp.bfloat16),
        "col",
        scatter_dimension=0,
        tiled=True,
    ).astype(jnp.float32)


def per_device(
    inputs, gate_weight, up_weight, down_weight, reward_head, upstream, labels, label_mask
):
    width = gate_weight.shape[1]
    gathered = gather_tokens(inputs)
    rows = gathered
    joined = lax.psum_scatter(
        jnp.concatenate(
            [
                jnp.dot(rows, gate_weight, preferred_element_type=jnp.float32),
                jnp.dot(rows, up_weight, preferred_element_type=jnp.float32),
            ],
            axis=1,
        ).astype(jnp.bfloat16),
        "row",
        scatter_dimension=0,
        tiled=True,
    ).astype(jnp.float32)
    gate = joined[:, :width]
    upper = joined[:, width:]
    sigmoid_gate = jax.nn.sigmoid(gate)
    hidden = (gate * sigmoid_gate * upper).astype(jnp.bfloat16)
    hidden_all = gather_hidden(hidden[None])[0]

    def output_term(start, count):
        return jnp.dot(hidden_all, down_weight, preferred_element_type=jnp.float32)

    mixed = column_total(output_term, inputs.shape[0])
    outcome = inputs.astype(jnp.float32) + mixed
    head_value = reward_head.astype(jnp.float32)
    partial_score = jnp.dot(outcome, head_value, precision=lax.Precision.HIGHEST)
    score = lax.psum(partial_score, "row")
    slope = (
        reward_weight
        * label_mask.astype(jnp.float32)
        * (jax.nn.sigmoid(score) - labels.astype(jnp.float32))
    )
    grad_out = upstream.astype(jnp.float32) + slope[:, None] * head_value[None, :]
    grad_mixed = grad_out.astype(jnp.bfloat16)
    grad_rows = gather_tokens(grad_mixed)
    rows = grad_rows
    grad_hidden = lax.psum_scatter(
        right_transpose(rows, down_weight).astype(jnp.bfloat16),
        "row",
        scatter_dimension=0,
        tiled=True,
    ).astype(jnp.float32)
    grad_gate = (grad_hidden * upper * sigmoid_gate * (1.0 + gate * (1.0 - sigmoid_gate))).astype(
        jnp.bfloat16
    )
    grad_upper = (grad_hidden * gate * sigmoid_gate).astype(jnp.bfloat16)
    grads_all = gather_hidden(jnp.stack([grad_gate, grad_upper]))

    def input_term(start, count):
        return right_transpose(grads_all[0], gate_weight) + right_transpose(grads_all[1], up_weight)

    input_grad = grad_out + column_total(input_term, inputs.shape[0])
    gate_grad, up_grad, down_grad = (
        lax.psum_scatter(
            transpose_product(gathered, grads_all[0]).astype(jnp.bfloat16),
            "dp",
            scatter_dimension=0,
            tiled=True,
        ).astype(jnp.float32),
        lax.psum_scatter(
            transpose_product(gathered, grads_all[1]).astype(jnp.bfloat16),
            "dp",
            scatter_dimension=0,
            tiled=True,
        ).astype(jnp.float32),
        lax.psum_scatter(
            transpose_product(hidden_all, grad_rows).astype(jnp.bfloat16),
            "dp",
            scatter_dimension=0,
            tiled=True,
        ).astype(jnp.float32),
    )
    return (gate_grad, up_grad, down_grad, input_grad)


def solution(mesh):
    in_specs = (
        P(("col", "dp"), "row"),
        P("row", "col"),
        P("row", "col"),
        P("col", "row"),
        P("row"),
        P(("col", "dp"), "row"),
        P(("col", "dp")),
        P(("col", "dp")),
    )
    out_specs = (
        P(("row", "dp"), "col"),
        P(("row", "dp"), "col"),
        P(("col", "dp"), "row"),
        P(("col", "dp"), "row"),
    )
    return jax.shard_map(
        per_device, mesh=mesh, in_specs=in_specs, out_specs=out_specs, check_vma=False
    )
```

profile of v0, /device:TPU:0, one launch (start us, length us, event | category | flops | bytes accessed | tf_op | source)
XLA Modules:
  0.0 650.1 jit_solution(301117565472167316)
XLA Ops:
  7.2 0.0 all-gather.6.cloned.1.call-start
  7.2 0.7 all-gather.6.cloned.1.call-update
  7.9 0.0 reduce-scatter.8.cloned.1.call-start
  7.9 50.3 %all-gather.6.cloned.1.call-done = bf16[512,2048]{1,0:T(8,128)(2,1)} async-done(((bf16[128,2048]{1,0:T(8,128)(2,1)}), bf16[512,2048]{1,0:T(8,128)(2,1)}) %all-gather.6.cloned.1.call-update) | async-done | bytes 2097168 | tf_op jit(solution)/shard_map/all_gather | solution.py:22
  58.2 13.6 %convolution_convert_fusion.4 = bf16[512,3584]{1,0:T(8,128)(2,1)S(1)} fusion(bf16[512,2048]{1,0:T(8,128)(2,1)} %all-gather.6.cloned.1.call-done, bf16[2048,3584]{1,0:T(8,128)(2,1)} %param.10), kind=kOutput, calls=%fused_computation.7 | convolution fusion | flops 7518027776 | bytes 20447232 | tf_op jit(solution)/shard_map/dot_general | solution.py:48
  71.9 12.3 %convolution_convert_fusion.5 = bf16[512,3584]{1,0:T(8,128)(2,1)} fusion(bf16[512,2048]{1,0:T(8,128)(2,1)S(1)} %copy-done.7, bf16[2048,3584]{1,0:T(8,128)(2,1)} %param.9), kind=kOutput, calls=%fused_computation.8 | convolution fusion | flops 7518027776 | bytes 20447232 | tf_op jit(solution)/shard_map/dot_general | solution.py:47
  84.2 6.1 pad_maximum_fusion
  90.2 0.0 reduce-scatter.8.cloned.1.call-update
  90.2 0.0 all-gather.12.cloned.1.call-start
  90.3 77.8 %reduce-scatter.8.cloned.1.call-done = bf16[128,7168]{1,0:T(8,128)(2,1)} async-done(((bf16[512,7168]{1,0:T(8,128)(2,1)}), bf16[128,7168]{1,0:T(8,128)(2,1)}) %reduce-scatter.8.cloned.1.call-update) | async-done | bytes 1835024 | tf_op jit(solution)/shard_map/reduce_scatter | solution.py:44
  168.1 1.9 convert_element_type.76
  170.0 1.8 copy-done
  171.8 1.4 multiply_convert_fusion
  173.2 0.0 all-gather.12.cloned.1.call-update
  173.3 0.0 reduce-scatter.10.cloned.1.call-start
  173.4 48.4 %all-gather.12.cloned.1.call-done = bf16[512,3584]{1,0:T(8,128)(2,1)} async-done(((bf16[128,3584]{1,0:T(8,128)(2,1)}), bf16[512,3584]{1,0:T(8,128)(2,1)}) %all-gather.12.cloned.1.call-update) | async-done | bytes 3670032 | tf_op jit(solution)/shard_map/all_gather | solution.py:26
  221.7 13.0 %convolution_convert_fusion.6 = bf16[512,2048]{1,0:T(8,128)(2,1)} fusion(bf16[512,3584]{1,0:T(8,128)(2,1)} %all-gather.12.cloned.1.call-done, bf16[3584,2048]{1,0:T(8,128)(2,1)} %param.11), kind=kOutput, calls=%fused_computation.14 | convolution fusion | flops 7517241344 | bytes 20447232 | tf_op jit(solution)/shard_map/dot_general | solution.py:63
  234.8 0.0 all-gather.8.cloned.1.call-start
  234.8 43.9 %reduce-scatter.10.cloned.1.call-done = bf16[128,2048]{1,0:T(8,128)(2,1)} async-done(((bf16[512,2048]{1,0:T(8,128)(2,1)}), bf16[128,2048]{1,0:T(8,128)(2,1)}) %reduce-scatter.10.cloned.1.call-update) | async-done | bytes 524304 | tf_op jit(solution)/shard_map/reduce_scatter | solution.py:30
  278.8 1.7 convolution_bitcast_fusion
  280.5 9.9 %psum.7 = f32[128]{0:T(128)S(1)} all-reduce(f32[128]{0:T(128)S(1)} %convolution_bitcast_fusion), channel_id=1, replica_groups=mesh['row'=4,'col'=4,'dp'=2] {'row'}, use_global_device_ids=true, to_apply=%region_2.0 | all-reduce | flops 128 | bytes 1024 | tf_op jit(solution)/shard_map/psum | solution.py:69
  290.4 1.0 fusion.12
  291.4 0.2 reduce-scatter.12.cloned.1.call-start
  291.6 43.3 %all-gather.8.cloned.1.call-done = bf16[512,2048]{1,0:T(8,128)(2,1)} async-done(((bf16[128,2048]{1,0:T(8,128)(2,1)}), bf16[512,2048]{1,0:T(8,128)(2,1)}) %all-gather.8.cloned.1.call-update) | async-done | bytes 2097168 | tf_op jit(solution)/shard_map/all_gather | solution.py:22
  334.9 12.9 %convolution_convert_fusion.3 = bf16[512,3584]{1,0:T(8,128)(2,1)} fusion(bf16[512,2048]{1,0:T(8,128)(2,1)} %all-gather.8.cloned.1.call-done, bf16[3584,2048]{1,0:T(8,128)(2,1)} %param.11), kind=kOutput, calls=%fused_computation.6 | convolution fusion | flops 7518027776 | bytes 20447232 | tf_op jit(solution)/shard_map/dot_general | solution.py:16
  347.9 0.0 all-gather.10.cloned.1.call-start
  347.9 47.2 %reduce-scatter.12.cloned.1.call-done = bf16[128,3584]{1,0:T(8,128)(2,1)} async-done(((bf16[512,3584]{1,0:T(8,128)(2,1)}), bf16[128,3584]{1,0:T(8,128)(2,1)}) %reduce-scatter.12.cloned.1.call-update) | async-done | bytes 917520 | tf_op jit(solution)/shard_map/reduce_scatter | solution.py:79
  395.1 3.1 fusion.14
  398.2 1.4 pad_maximum_fusion.1
  399.6 0.0 reduce-scatter.20.cloned.1.call-start
  399.7 79.0 %all-gather.10.cloned.1.call-done = bf16[2,512,3584]{2,1,0:T(8,128)(2,1)} async-done(((bf16[2,128,3584]{2,1,0:T(8,128)(2,1)}), bf16[2,512,3584]{2,1,0:T(8,128)(2,1)}) %all-gather.10.cloned.1.call-update) | async-done | bytes 7340048 | tf_op jit(solution)/shard_map/all_gather | solution.py:26
  478.7 15.4 %fusion.2 = f32[512,2048]{1,0:T(8,128)} fusion(bf16[2048,3584]{1,0:T(8,128)(2,1)} %param.9, bf16[2,512,3584]{2,1,0:T(8,128)(2,1)} %all-gather.10.cloned.1.call-done), kind=kOutput, calls=%fused_computation.12 | convolution fusion | flops 7516192768 | bytes 22544384 | tf_op jit(solution)/shard_map/dot_general | solution.py:16
  494.1 12.8 %add_convert_fusion = bf16[512,2048]{1,0:T(8,128)(2,1)} fusion(f32[512,2048]{1,0:T(8,128)} %fusion.2, bf16[2048,3584]{1,0:T(8,128)(2,1)} %param.10, bf16[2,512,3584]{2,1,0:T(8,128)(2,1)S(1)} %copy-done.6), kind=kOutput, calls=%fused_computation.9 | convolution fusion | flops 7518289920 | bytes 24641536 | tf_op jit(solution)/shard_map/dot_general | solution.py:16
  507.0 0.3 reduce-scatter.18.cloned.1.call-start
  507.3 13.2 %convolution_convert_fusion = bf16[3584,2048]{1,0:T(8,128)(2,1)} fusion(bf16[512,3584]{1,0:T(8,128)(2,1)} %all-gather.12.cloned.1.call-done, bf16[512,2048]{1,0:T(8,128)(2,1)S(1)} %copy-done.9), kind=kOutput, calls=%fused_computation | convolution fusion | flops 7523532800 | bytes 20447232 | tf_op jit(solution)/shard_map/dot_general | solution.py:10
  520.4 0.0 reduce-scatter.14.cloned.1.call-start
  520.5 1.5 copy-done.8
  522.0 13.2 %fusion = bf16[2048,3584]{0,1:T(8,128)(2,1)} fusion(bf16[512,2048]{1,0:T(8,128)(2,1)S(1)} %copy-done.8, bf16[2,512,3584]{2,1,0:T(8,128)(2,1)} %all-gather.10.cloned.1.call-done), kind=kOutput, calls=%fused_computation.3 | convolution fusion | flops 7523532800 | bytes 20447232 | tf_op jit(solution)/shard_map/dot_general | solution.py:10
  535.2 0.3 reduce-scatter.16.cloned.1.call-start
  535.5 13.1 %fusion.1 = bf16[2048,3584]{0,1:T(8,128)(2,1)} fusion(bf16[512,2048]{1,0:T(8,128)(2,1)S(1)} %copy-done.8, bf16[2,512,3584]{2,1,0:T(8,128)(2,1)} %all-gather.10.cloned.1.call-done), kind=kOutput, calls=%fused_computation.4 | convolution fusion | flops 7523532800 | bytes 20447232 | tf_op jit(solution)/shard_map/dot_general | solution.py:10
  548.7 2.3 reduce-scatter.20.cloned.1.call-done
  551.0 2.3 convert_add_fusion
  553.3 23.9 %reduce-scatter.18.cloned.1.call-done = bf16[1792,2048]{1,0:T(8,128)(2,1)} async-done(((bf16[3584,2048]{1,0:T(8,128)(2,1)}), bf16[1792,2048]{1,0:T(8,128)(2,1)}) %reduce-scatter.18.cloned.1.call-update) | async-done | bytes 7340048 | tf_op jit(solution)/shard_map/reduce_scatter | solution.py:108
  577.1 10.6 %convert_element_type.94 = f32[1792,2048]{1,0:T(8,128)} convert(bf16[1792,2048]{1,0:T(8,128)(2,1)} %reduce-scatter.18.cloned.1.call-done) | non-fusion elementwise | flops 3670016 | bytes 22020096 | tf_op jit(solution)/shard_map/convert_element_type | solution.py:113
  587.7 17.4 %reduce-scatter.14.cloned.1.call-done = bf16[1024,3584]{0,1:T(8,128)(2,1)} async-done(((bf16[2048,3584]{0,1:T(8,128)(2,1)}), bf16[1024,3584]{0,1:T(8,128)(2,1)}) %reduce-scatter.14.cloned.1.call-update) | async-done | bytes 7340048 | tf_op jit(solution)/shard_map/reduce_scatter | solution.py:96
  605.0 11.0 %copy.12 = f32[1024,3584]{1,0:T(8,128)} copy(bf16[1024,3584]{0,1:T(8,128)(2,1)} %reduce-scatter.14.cloned.1.call-done) | data formatting | bytes 22020096
  616.1 16.5 %reduce-scatter.16.cloned.1.call-done = bf16[1024,3584]{0,1:T(8,128)(2,1)} async-done(((bf16[2048,3584]{0,1:T(8,128)(2,1)}), bf16[1024,3584]{0,1:T(8,128)(2,1)}) %reduce-scatter.16.cloned.1.call-update) | async-done | bytes 7340048 | tf_op jit(solution)/shard_map/reduce_scatter | solution.py:102
  632.5 11.0 %copy.13 = f32[1024,3584]{1,0:T(8,128)} copy(bf16[1024,3584]{0,1:T(8,128)(2,1)} %reduce-scatter.16.cloned.1.call-done) | data formatting | bytes 22020096
  (29 shorter events, 0.2 us)
Async XLA Ops:
  7.2 51.1 %all-gather.6.cloned.1.call-start = ((), (), s32[]{:S(2)}) async-start(), calls=%async_computation.7 | async-start | bytes 2621440 | tf_op jit(solution)/shard_map/all_gather | solution.py:22
  7.9 160.2 %reduce-scatter.8.cloned.1.call-start = ((), (), s32[]{:S(2)}) async-start(), calls=%async_computation.8 | async-start | bytes 9175040 | tf_op jit(solution)/shard_map/reduce_scatter | solution.py:44
  58.2 13.6 %copy-start.7 = (bf16[512,2048]{1,0:T(8,128)(2,1)S(1)}, bf16[512,2048]{1,0:T(8,128)(2,1)}, u32[]{:S(2)}) copy-start(bf16[512,2048]{1,0:T(8,128)(2,1)} %all-gather.6.cloned.1.call-done) | copy-start | bytes 6291460
  90.2 131.5 %all-gather.12.cloned.1.call-start = ((), (), s32[]{:S(2)}) async-start(), calls=%async_computation.17 | async-start | bytes 4587520 | tf_op jit(solution)/shard_map/all_gather | solution.py:26
  170.0 1.8 copy-start
  173.2 61.6 %copy-start.3 = (bf16[2048]{0:T(1024)(128)(2,1)S(1)}, bf16[2048]{0:T(1024)(128)(2,1)}, u32[]{:S(2)}) copy-start(bf16[2048]{0:T(1024)(128)(2,1)} %param.12) | copy-start | bytes 12292
  173.3 105.5 %copy-start.2 = (bf16[128,2048]{1,0:T(8,128)(2,1)S(1)}, bf16[128,2048]{1,0:T(8,128)(2,1)}, u32[]{:S(2)}) copy-start(bf16[128,2048]{1,0:T(8,128)(2,1)} %param.8) | copy-start | bytes 1572868
  173.3 117.1 %copy-start.4 = (s32[128]{0:T(128)S(1)}, s32[128]{0:T(128)}, u32[]{:S(2)}) copy-start(s32[128]{0:T(128)} %param.14) | copy-start | bytes 1540
  173.3 117.1 %copy-start.5 = (s32[128]{0:T(128)S(1)}, s32[128]{0:T(128)}, u32[]{:S(2)}) copy-start(s32[128]{0:T(128)} %param.15) | copy-start | bytes 1540
  173.3 117.1 %copy-start.1 = (bf16[128,2048]{1,0:T(8,128)(2,1)S(1)}, bf16[128,2048]{1,0:T(8,128)(2,1)}, u32[]{:S(2)}) copy-start(bf16[128,2048]{1,0:T(8,128)(2,1)} %param.13) | copy-start | bytes 1572868
  173.3 105.5 %reduce-scatter.10.cloned.1.call-start = ((), (), s32[]{:S(2)}) async-start(), calls=%async_computation.9 | async-start | bytes 2621440 | tf_op jit(solution)/shard_map/reduce_scatter | solution.py:30
  234.8 100.2 %all-gather.8.cloned.1.call-start = ((), (), s32[]{:S(2)}) async-start(), calls=%async_computation.10 | async-start | bytes 2621440 | tf_op jit(solution)/shard_map/all_gather | solution.py:22
  291.4 103.7 %reduce-scatter.12.cloned.1.call-start = ((), (), s32[]{:S(2)}) async-start(), calls=%async_computation.11 | async-start | bytes 4587520 | tf_op jit(solution)/shard_map/reduce_scatter | solution.py:79
  347.9 130.8 %all-gather.10.cloned.1.call-start = ((), (), s32[]{:S(2)}) async-start(), calls=%async_computation.12 | async-start | bytes 9175040 | tf_op jit(solution)/shard_map/all_gather | solution.py:26
  399.6 151.4 %reduce-scatter.20.cloned.1.call-start = ((), (), s32[]{:S(2)}) async-start(), calls=%async_computation.16 | async-start | bytes 2621440 | tf_op jit(solution)/shard_map/reduce_scatter | solution.py:30
  478.7 15.4 %copy-start.6 = (bf16[2,512,3584]{2,1,0:T(8,128)(2,1)S(1)}, bf16[2,512,3584]{2,1,0:T(8,128)(2,1)}, u32[]{:S(2)}) copy-start(bf16[2,512,3584]{2,1,0:T(8,128)(2,1)} %all-gather.10.cloned.1.call-done) | copy-start | bytes 22020100
  494.1 13.1 %copy-start.9 = (bf16[512,2048]{1,0:T(8,128)(2,1)S(1)}, bf16[512,2048]{1,0:T(8,128)(2,1)}, u32[]{:S(2)}) copy-start(bf16[512,2048]{1,0:T(8,128)(2,1)} %all-gather.8.cloned.1.call-done) | copy-start | bytes 6291460
  507.0 70.1 %reduce-scatter.18.cloned.1.call-start = ((), (), s32[]{:S(2)}) async-start(), calls=%async_computation.15 | async-start | bytes 22020096 | tf_op jit(solution)/shard_map/reduce_scatter | solution.py:108
  520.4 1.6 copy-start.8
  520.4 84.6 %reduce-scatter.14.cloned.1.call-start = ((), (), s32[]{:S(2)}) async-start(), calls=%async_computation.13 | async-start | bytes 22020096 | tf_op jit(solution)/shard_map/reduce_scatter | solution.py:96
  535.2 97.3 %reduce-scatter.16.cloned.1.call-start = ((), (), s32[]{:S(2)}) async-start(), calls=%async_computation.14 | async-start | bytes 22020096 | tf_op jit(solution)/shard_map/reduce_scatter | solution.py:102
Sparse Core Ops, SparseCore 0:
  9.6 48.6 all-gather.5
  90.4 77.6 reduce-scatter.7
  173.4 48.3 all-gather.11
  234.9 43.8 reduce-scatter.9
  291.5 43.3 all-gather.7
  348.0 47.0 reduce-scatter.11
  399.8 78.8 all-gather.9
  507.1 43.8 reduce-scatter.19
  553.9 23.1 reduce-scatter.17
  579.8 25.1 reduce-scatter.13
  607.3 25.1 reduce-scatter.15
where the time goes:
time: 651 us; the launch traced here: 650 us
  waiting for transfers between devices  451 us (69%)
  matrix products  121 us (19%)
  other arithmetic  27.7 us (4%)
  local copies, waits for them, and re-layouts  25.5 us (4%)
  between operations  14 us (2%)
  blocking collectives  9.88 us (2%)
    all_gather x2, waiting for transfers between devices, gather_hidden(): return lax.all_gather(stacked, 'row', axis=1, tiled=True)  127 us
    all_gather x2, waiting for transfers between devices, gather_tokens(): return lax.all_gather(block, 'col', axis=0, tiled=True)  93.6 us
    reduce_scatter x1, waiting for transfers between devices, per_device(): lax.psum_scatter(jnp.concatenate([jnp.dot(rows, gate_weight, preferred_el...  77.8 us
    reduce_scatter x1, waiting for transfers between devices, per_device(): lax.psum_scatter(right_transpose(rows, down_weight).astype(jnp.bfloat16),...  47.2 us
    reduce_scatter x2, waiting for transfers between devices, column_total(): lax.psum_scatter(term_fn(jnp.int32(0), count_rows * lax.axis_size('col'))...  46.3 us
    dot_general x3, matrix products, right_transpose(): lax.dot_general(left, right, (((1,), (1,)), ((), ())), preferred_element_...  41.2 us
    dot_general x3, matrix products, transpose_product(): lax.dot_general(left, right, (((0,), (0,)), ((), ())), preferred_element_...  39.4 us
    unnamed x23, local copies, waits for them, and re-layouts  25.5 us
  transfers between devices with their start and end apart: 11, of which 11 were waited for; matrix products, arithmetic and copies ran while one was open for 10% of the time, Pallas kernels for 0%

commit v1 on v0

v1 whole, which is shorter than its diff:
```python
import jax
import jax.numpy as jnp
from jax import lax
from jax.sharding import PartitionSpec as P

reward_weight = 8.0
CHUNKS = 2
F32 = jnp.float32
BF16 = jnp.bfloat16


def transpose_product(left, right):
    return lax.dot_general(left, right, (((0,), (0,)), ((), ())), preferred_element_type=F32)


def right_transpose(left, right):
    return lax.dot_general(left, right, (((1,), (1,)), ((), ())), preferred_element_type=F32)


def swap(value, axis, distance):
    size = lax.axis_size(axis)
    return lax.ppermute(value, axis, [(i, i ^ distance) for i in range(size)])


def bit_orders():
    bits = (lax.axis_size("row") - 1).bit_length()
    return list(range(bits)), list(reversed(range(bits)))


def row_scatter(value, order):
    size = lax.axis_size("row")
    me = lax.axis_index("row")
    bits = (size - 1).bit_length()
    count = value.shape[0] // size
    total = value.reshape((2,) * bits + (count, value.shape[1]))
    left = list(reversed(range(bits)))
    for bit in order:
        axis = left.index(bit)
        left.remove(bit)
        mine = (me >> bit) & 1
        keep = lax.dynamic_index_in_dim(total, mine, axis, keepdims=False)
        send = lax.dynamic_index_in_dim(total, 1 - mine, axis, keepdims=False)
        total = keep.astype(F32) + swap(send.astype(BF16), "row", 1 << bit).astype(F32)
    return total


def row_gather(value, order):
    size = lax.axis_size("row")
    me = lax.axis_index("row")
    bits = (size - 1).bit_length()
    held = value
    left = []
    for bit in order:
        axis = len([b for b in left if b > bit])
        other = swap(held, "row", 1 << bit)
        mine = (me >> bit) & 1
        low = jnp.where(mine == 0, held, other)
        high = jnp.where(mine == 0, other, held)
        held = jnp.stack([low, high], axis=axis)
        left = sorted(left + [bit], reverse=True)
    return held.reshape((size * value.shape[0],) + value.shape[1:])


def row_sum(value):
    total = value
    for distance in range(1, lax.axis_size("row")):
        total = total + swap(value, "row", distance)
    return total


def col_gather(value):
    size = lax.axis_size("col")
    me = lax.axis_index("col")
    up, down = [value], [value]
    for step in range(1, size):
        up.append(lax.ppermute(up[-1], "col", [(i, i + 1) for i in range(step - 1, size - 1)]))
        down.append(lax.ppermute(down[-1], "col", [(i, i - 1) for i in range(1, size - step + 1)]))
    blocks = [value]
    for k in range(1, size):
        blocks.append(jnp.where(me >= k, up[k], down[size - k]))
    return jnp.concatenate(blocks, axis=0)


def col_scatter(value):
    size = lax.axis_size("col")
    blocks = jnp.split(value, size, axis=0)
    up, down = blocks[1], blocks[size - 1]
    for step in range(1, size):
        if step > 1:
            up = (up.astype(F32) + blocks[step].astype(F32)).astype(BF16)
            down = (down.astype(F32) + blocks[size - step].astype(F32)).astype(BF16)
        up = lax.ppermute(up, "col", [(i, i + 1) for i in range(step)])
        down = lax.ppermute(down, "col", [(i, i - 1) for i in range(size - step, size)])
    return blocks[0].astype(F32) + (up.astype(F32) + down.astype(F32))


def with_peer_half(value, axis_halves):
    d = lax.axis_index("dp")
    half = value.shape[1] // axis_halves
    mine = lax.dynamic_slice_in_dim(value, d * half, half, axis=1)
    send = lax.dynamic_slice_in_dim(value, (1 - d) * half, half, axis=1)
    return jnp.concatenate([mine, swap(send, "dp", 1)], axis=0)


def with_peer(value):
    return jnp.concatenate([value, swap(value, "dp", 1)], axis=0)


def per_device(
    inputs, gate_weight, up_weight, down_weight, reward_head, upstream, labels, label_mask
):
    head_value = reward_head.astype(F32)
    low_first, high_first = bit_orders()
    count = inputs.shape[0] // CHUNKS
    middle = gate_weight.shape[1] // 2

    def part(array, c):
        return array[c * count:(c + 1) * count]

    gathered = [col_gather(part(inputs, c)) for c in range(CHUNKS)]
    gate_grad = up_grad = down_grad = None
    input_grads = []
    for c in range(CHUNKS):
        rows = gathered[c]
        gate = row_scatter(
            jnp.dot(rows, gate_weight, preferred_element_type=F32).astype(BF16), low_first
        )
        upper = row_scatter(
            jnp.dot(rows, up_weight, preferred_element_type=F32).astype(BF16), high_first
        )
        sigmoid_gate = jax.nn.sigmoid(gate)
        hidden = (gate * sigmoid_gate * upper).astype(BF16)
        hidden_all = jnp.concatenate(
            [
                row_gather(hidden[:, :middle], low_first),
                row_gather(hidden[:, middle:], high_first),
            ],
            axis=1,
        )
        mixed = col_scatter(
            jnp.dot(hidden_all, down_weight, preferred_element_type=F32).astype(BF16)
        )
        outcome = part(inputs, c).astype(F32) + mixed
        score = row_sum(jnp.sum(outcome * head_value[None, :], axis=1))
        slope = (
            reward_weight
            * part(label_mask, c).astype(F32)
            * (jax.nn.sigmoid(score) - part(labels, c).astype(F32))
        )
        grad_out = part(upstream, c).astype(F32) + slope[:, None] * head_value[None, :]
        grad_rows = col_gather(grad_out.astype(BF16))
        product = right_transpose(grad_rows, down_weight).astype(BF16)
        grad_hidden = jnp.concatenate(
            [
                row_scatter(product[:, :middle], low_first),
                row_scatter(product[:, middle:], high_first),
            ],
            axis=1,
        )
        grad_gate = (
            grad_hidden * upper * sigmoid_gate * (1.0 + gate * (1.0 - sigmoid_gate))
        ).astype(BF16)
        grad_upper = (grad_hidden * gate * sigmoid_gate).astype(BF16)
        gate_all = row_gather(grad_gate, low_first)
        upper_all = row_gather(grad_upper, high_first)
        input_term = right_transpose(gate_all, gate_weight) + right_transpose(upper_all, up_weight)
        input_grads.append(grad_out + col_scatter(input_term.astype(BF16)))

        rows_both = with_peer_half(rows, 2)
        down_c = transpose_product(with_peer_half(hidden_all, 2), with_peer(grad_rows))
        gate_c = transpose_product(rows_both, with_peer(gate_all))
        up_c = transpose_product(rows_both, with_peer(upper_all))
        down_grad = down_c if down_grad is None else down_grad + down_c
        gate_grad = gate_c if gate_grad is None else gate_grad + gate_c
        up_grad = up_c if up_grad is None else up_grad + up_c
    return (gate_grad, up_grad, down_grad, jnp.concatenate(input_grads, axis=0))


def solution(mesh):
    in_specs = (
        P(("col", "dp"), "row"),
        P("row", "col"),
        P("row", "col"),
        P("col", "row"),
        P("row"),
        P(("col", "dp"), "row"),
        P(("col", "dp")),
        P(("col", "dp")),
    )
    out_specs = (
        P(("row", "dp"), "col"),
        P(("row", "dp"), "col"),
        P(("col", "dp"), "row"),
        P(("col", "dp"), "row"),
    )
    return jax.shard_map(
        per_device, mesh=mesh, in_specs=in_specs, out_specs=out_specs, check_vma=False
    )
```

time: 651 us -> 581 us (0.89); the launches traced: 650 us -> 573 us
  waiting for transfers between devices: 451 us -> 187 us
  starting transfers between devices: 1.11 us -> 158 us
  matrix products: 121 us -> 174 us
  between operations: 14 us -> 3 us
  blocking collectives: 9.88 us -> 0 us
  local copies, waits for them, and re-layouts: 25.5 us -> 18.7 us
    reduce_scatter x7 -> x0, waiting for transfers between devices: 229 us -> none  [the longest x1 77.8 us: per_device(): lax.psum_scatter(jnp.concatenate([jnp.dot(rows, gate_weight, preferred_el...]
    all_gather x4 -> x0, waiting for transfers between devices: 221 us -> none  [the longest x2 127 us: gather_hidden(): return lax.all_gather(stacked, 'row', axis=1, tiled=True)]
    ppermute x0 -> x96, waiting for transfers between devices: none -> 187 us  [the longest x48 137 us: swap(): return lax.ppermute(value, axis, [(i, i ^ distance) for i in range(size)])]
    ppermute x0 -> x96, starting transfers between devices: none -> 158 us  [the longest x12 55 us: col_scatter(): up = lax.ppermute(up, 'col', [(i, i + 1) for i in range(step)])]
    dot_general x3 -> x6, matrix products: 41.2 us -> 68.6 us  [right_transpose(): lax.dot_general(left, right, (((1,), (1,)), ((), ())), preferred_element_...]
    dot_general x3 -> x6, matrix products: 39.4 us -> 65.4 us  [transpose_product(): lax.dot_general(left, right, (((0,), (0,)), ((), ())), preferred_element_...]
    unnamed x23 -> x158, local copies, waits for them, and re-layouts: 25.5 us -> 4.35 us
    psum x1 -> x0, blocking collectives: 9.88 us -> none  [per_device(): score = lax.psum(partial_score, 'row')]
  transfers between devices with their start and end apart: 11 -> 96, of which waited for: 11 -> 38; matrix products, arithmetic and copies ran while one was open for 10% -> 34% of each run, Pallas kernels for 0% -> 0%
where the time goes in v1:
time: 581 us; the launch traced here: 573 us
  waiting for transfers between devices  187 us (32%)
  matrix products  174 us (30%)
  starting transfers between devices  158 us (27%)
  other arithmetic  32.9 us (6%)
  local copies, waits for them, and re-layouts  18.7 us (3%)
    ppermute x48, waiting for transfers between devices, swap(): return lax.ppermute(value, axis, [(i, i ^ distance) for i in range(size)])  137 us
    dot_general x6, matrix products, right_transpose(): lax.dot_general(left, right, (((1,), (1,)), ((), ())), preferred_element_...  68.6 us
    dot_general x6, matrix products, transpose_product(): lax.dot_general(left, right, (((0,), (0,)), ((), ())), preferred_element_...  65.4 us
    ppermute x12, starting transfers between devices, col_scatter(): up = lax.ppermute(up, 'col', [(i, i + 1) for i in range(step)])  55 us
    ppermute x48, starting transfers between devices, swap(): return lax.ppermute(value, axis, [(i, i ^ distance) for i in range(size)])  40.2 us
    ppermute x12, waiting for transfers between devices, col_gather(): lax.ppermute(down[-1], 'col', [(i, i - 1) for i in range(1, size - step +...  28.8 us
    ppermute x12, starting transfers between devices, col_gather(): lax.ppermute(up[-1], 'col', [(i, i + 1) for i in range(step - 1, size - 1)])  26.1 us
    ppermute x12, starting transfers between devices, col_gather(): lax.ppermute(down[-1], 'col', [(i, i - 1) for i in range(1, size - step +...  25.6 us
  transfers between devices with their start and end apart: 96, of which 38 were waited for; matrix products, arithmetic and copies ran while one was open for 34% of the time, Pallas kernels for 0%

profile of v1, /device:TPU:0, one launch (start us, length us, event | category | flops | bytes accessed | tf_op | source)
XLA Modules:
  0.0 573.0 jit_solution(10517775019944952229)
XLA Ops:
  3.0 5.6 collective-permute-start.37
  9.9 4.6 collective-permute-start
  27.0 4.5 collective-permute-done.2
  33.6 7.5 %collective-permute-done.3 = bf16[64,2048]{1,0:T(8,128)(2,1)S(1)} collective-permute-done((bf16[64,2048]{1,0:T(8,128)(2,1)S(1)}, bf16[64,2048]{1,0:T(8,128)(2,1)S(1)}, u32[]{:S(2)}, u32[]{:S(2)}) %collective-permute-start.3) | collective-permute-done | bytes 262176 | tf_op jit(solution)/shard_map/ppermute | solution.py:77
  41.2 9.3 %convolution_convert_fusion.5 = bf16[256,3584]{1,0:T(8,128)(2,1)S(1)} fusion(bf16[2048,3584]{1,0:T(8,128)(2,1)} %param.9, bf16[64,2048]{1,0:T(8,128)(2,1)S(1)} %broadcast_select_fusion.3, bf16[64,2048]{1,0:T(8,128)(2,1)S(1)} %broadcast_select_fusion.7, bf16[64,2048]{1,0:T(8,128)(2,1)S(1)} %broadcast_select_fusion.11, bf16[64,2048]{1,0:T(8,128)(2,1)S(1)} %get-tuple-element.99), kind=kOutput, calls=%fused_computation.8 | convolution fusion | flops 3763208192 | bytes 17563648 | tf_op jit(solution)/shard_map/dot_general | solution.py:126
  50.5 9.3 %convolution_convert_fusion.4 = bf16[256,3584]{1,0:T(8,128)(2,1)S(1)} fusion(bf16[2048,3584]{1,0:T(8,128)(2,1)} %param.10, bf16[64,2048]{1,0:T(8,128)(2,1)S(1)} %broadcast_select_fusion.3, bf16[64,2048]{1,0:T(8,128)(2,1)S(1)} %broadcast_select_fusion.7, bf16[64,2048]{1,0:T(8,128)(2,1)S(1)} %broadcast_select_fusion.11, bf16[64,2048]{1,0:T(8,128)(2,1)S(1)} %get-tuple-element.99), kind=kOutput, calls=%fused_computation.7 | convolution fusion | flops 3763208192 | bytes 17563648 | tf_op jit(solution)/shard_map/dot_general | solution.py:129
  60.0 4.0 convolution_convert_fusion.2
  64.1 9.1 %convolution_convert_fusion.1 = bf16[256,3584]{1,0:T(8,128)(2,1)S(1)} fusion(bf16[2048,3584]{1,0:T(8,128)(2,1)} %param.10, bf16[64,2048]{1,0:T(8,128)(2,1)S(1)} %broadcast_select_fusion.1, bf16[64,2048]{1,0:T(8,128)(2,1)S(1)} %broadcast_select_fusion.5, bf16[64,2048]{1,0:T(8,128)(2,1)S(1)} %broadcast_select_fusion.9, bf16[64,2048]{1,0:T(8,128)(2,1)S(1)} %get-tuple-element.98), kind=kOutput, calls=%fused_computation.4 | convolution fusion | flops 3763208192 | bytes 17563648 | tf_op jit(solution)/shard_map/dot_general | solution.py:129
  77.8 18.8 %collective-permute-done.7 = bf16[2,64,3584]{2,1,0:T(8,128)(2,1)S(1)} collective-permute-done((bf16[2,64,3584]{2,1,0:T(8,128)(2,1)S(1)}, bf16[2,64,3584]{2,1,0:T(8,128)(2,1)S(1)}, u32[]{:S(2)}, u32[]{:S(2)}) %collective-permute-start.7) | collective-permute-done | bytes 917536 | tf_op jit(solution)/shard_map/ppermute | solution.py:22
  100.6 15.7 %collective-permute-done.44 = bf16[2,64,3584]{2,1,0:T(8,128)(2,1)S(1)} collective-permute-done((bf16[2,64,3584]{2,1,0:T(8,128)(2,1)S(1)}, bf16[2,64,3584]{2,1,0:T(8,128)(2,1)S(1)}, u32[]{:S(2)}, u32[]{:S(2)}) %collective-permute-start.44) | collective-permute-done | bytes 917536 | tf_op jit(solution)/shard_map/ppermute | solution.py:22
  120.3 7.6 %collective-permute-done.8 = bf16[64,3584]{1,0:T(8,128)(2,1)S(1)} collective-permute-done((bf16[64,3584]{1,0:T(8,128)(2,1)S(1)}, bf16[64,3584]{1,0:T(8,128)(2,1)S(1)}, u32[]{:S(2)}, u32[]{:S(2)}) %collective-permute-start.8) | collective-permute-done | bytes 458784 | tf_op jit(solution)/shard_map/ppermute | solution.py:22
  130.7 7.1 %collective-permute-done.45 = bf16[64,3584]{1,0:T(8,128)(2,1)S(1)} collective-permute-done((bf16[64,3584]{1,0:T(8,128)(2,1)S(1)}, bf16[64,3584]{1,0:T(8,128)(2,1)S(1)}, u32[]{:S(2)}, u32[]{:S(2)}) %collective-permute-start.45) | collective-permute-done | bytes 458784 | tf_op jit(solution)/shard_map/ppermute | solution.py:22
  150.6 6.0 %collective-permute-done.14 = bf16[2,64,1792]{2,1,0:T(8,128)(2,1)S(1)} collective-permute-done((bf16[2,64,1792]{2,1,0:T(8,128)(2,1)S(1)}, bf16[2,64,1792]{2,1,0:T(8,128)(2,1)S(1)}, u32[]{:S(2)}, u32[]{:S(2)}) %collective-permute-start.14) | collective-permute-done | bytes 458784 | tf_op jit(solution)/shard_map/ppermute | solution.py:22
  157.6 3.9 convolution_convert_fusion.7
  176.5 4.4 collective-permute-start.53
  182.6 8.4 %collective-permute-start.17 = (bf16[64,2048]{1,0:T(8,128)(2,1)}, bf16[64,2048]{1,0:T(8,128)(2,1)}, u32[]{:S(2)}, u32[]{:S(2)}) collective-permute-start(bf16[64,2048]{1,0:T(8,128)(2,1)} %get-tuple-element.64), channel_id=1, source_target_pairs={{0,2},{2,4},{4,6},{1,3},{3,5},{5,7},{8,10},{10,12},{12,14},{9,11},... | collective-permute-start | bytes 786440 | tf_op jit(solution)/shard_map/ppermute | solution.py:92
  193.2 6.9 %collective-permute-start.54 = (bf16[64,2048]{1,0:T(8,128)(2,1)}, bf16[64,2048]{1,0:T(8,128)(2,1)}, u32[]{:S(2)}, u32[]{:S(2)}) collective-permute-start(bf16[64,2048]{1,0:T(8,128)(2,1)} %get-tuple-element.58), channel_id=1, source_target_pairs={{0,2},{2,4},{4,6},{1,3},{3,5},{5,7},{8,10},{10,12},{12,14},{9,11},... | collective-permute-start | bytes 786440 | tf_op jit(solution)/shard_map/ppermute | solution.py:92
  203.6 5.1 collective-permute-done.57
  225.0 5.2 collective-permute-start.24
  234.2 11.2 %collective-permute-start.63 = (bf16[64,2048]{1,0:T(8,128)(2,1)S(1)}, bf16[64,2048]{1,0:T(8,128)(2,1)S(1)}, u32[]{:S(2)}, u32[]{:S(2)}) collective-permute-start(bf16[64,2048]{1,0:T(8,128)(2,1)S(1)} %collective-permute-done.62), channel_id=1, source_target_pairs={{2,0},{4,2},{3,1},{5,3},{10,8},{12,10},{11,9},{13,11},{18,16},{20,... | collective-permute-start | bytes 786440 | tf_op jit(solution)/shard_map/ppermute | solution.py:77
  261.7 5.3 collective-permute-done.64
  271.3 10.7 %convolution_convert_fusion = bf16[256,3584]{1,0:T(8,128)(2,1)} fusion(bf16[3584,2048]{1,0:T(8,128)(2,1)} %param.11, bf16[64,2048]{1,0:T(8,128)(2,1)} %get-tuple-element.15, bf16[64,2048]{1,0:T(8,128)(2,1)} %get-tuple-element.17, bf16[64,2048]{1,0:T(8,128)(2,1)} %get-tuple-element.19, bf16[64,2048]{1,0:T(8,128)(2,1)} %copy-done.52), kind=kOutput, calls=%fused_computation.3 | convolution fusion | flops 3763208192 | bytes 17563648 | tf_op jit(solution)/shard_map/dot_general | solution.py:17
  293.9 10.7 %convolution_convert_fusion.3 = bf16[256,3584]{1,0:T(8,128)(2,1)} fusion(bf16[3584,2048]{1,0:T(8,128)(2,1)} %param.11, bf16[64,2048]{1,0:T(8,128)(2,1)} %get-tuple-element.7, bf16[64,2048]{1,0:T(8,128)(2,1)} %get-tuple-element.9, bf16[64,2048]{1,0:T(8,128)(2,1)} %get-tuple-element.11, bf16[64,2048]{1,0:T(8,128)(2,1)S(1)} %get-tuple-element.13), kind=kOutput, calls=%fused_computation.6 | convolution fusion | flops 3763208192 | bytes 17563648 | tf_op jit(solution)/shard_map/dot_general | solution.py:17
  310.1 6.8 %collective-permute-done.30 = bf16[2,64,1792]{2,1,0:T(8,128)(2,1)S(1)} collective-permute-done((bf16[2,64,1792]{2,1,0:T(8,128)(2,1)S(1)}, bf16[2,64,1792]{2,1,0:T(8,128)(2,1)S(1)}, u32[]{:S(2)}, u32[]{:S(2)}) %collective-permute-start.30) | collective-permute-done | bytes 458784 | tf_op jit(solution)/shard_map/ppermute | solution.py:22
  318.1 7.1 %collective-permute-done.68 = bf16[64,1792]{1,0:T(8,128)(2,1)S(1)} collective-permute-done((bf16[64,1792]{1,0:T(8,128)(2,1)S(1)}, bf16[64,1792]{1,0:T(8,128)(2,1)S(1)}, u32[]{:S(2)}, u32[]{:S(2)}) %collective-permute-start.68) | collective-permute-done | bytes 229408 | tf_op jit(solution)/shard_map/ppermute | solution.py:22
  325.9 6.3 %collective-permute-done.70 = bf16[64,1792]{1,0:T(8,128)(2,1)S(1)} collective-permute-done((bf16[64,1792]{1,0:T(8,128)(2,1)S(1)}, bf16[64,1792]{1,0:T(8,128)(2,1)S(1)}, u32[]{:S(2)}, u32[]{:S(2)}) %collective-permute-start.70) | collective-permute-done | bytes 229408 | tf_op jit(solution)/shard_map/ppermute | solution.py:22
  333.4 4.8 collective-permute-done.31
  338.5 5.8 %collective-permute-done.33 = bf16[64,1792]{1,0:T(8,128)(2,1)S(1)} collective-permute-done((bf16[64,1792]{1,0:T(8,128)(2,1)S(1)}, bf16[64,1792]{1,0:T(8,128)(2,1)S(1)}, u32[]{:S(2)}, u32[]{:S(2)}) %collective-permute-start.33) | collective-permute-done | bytes 229408 | tf_op jit(solution)/shard_map/ppermute | solution.py:22
  348.3 9.0 %fusion.19 = f32[1792,2048]{1,0:T(8,128)} fusion(bf16[512,2048]{1,0:T(8,128)(2,1)S(1)} %constant_dynamic-update-slice_fusion.5, bf16[256,1792]{1,0:T(8,128)(2,1)} %collective-permute-done.82, bf16[256,1792]{1,0:T(8,128)(2,1)S(1)} %copy-done.60), kind=kOutput, calls=%fused_computation.46 | convolution fusion | flops 3761766400 | bytes 18612224 | tf_op jit(solution)/shard_map/dot_general | solution.py:13
  361.3 5.7 collective-permute-done.74
  372.2 18.2 %collective-permute-done.78 = bf16[2,64,3584]{2,1,0:T(8,128)(2,1)S(1)} collective-permute-done((bf16[2,64,3584]{2,1,0:T(8,128)(2,1)S(1)}, bf16[2,64,3584]{2,1,0:T(8,128)(2,1)S(1)}, u32[]{:S(2)}, u32[]{:S(2)}) %collective-permute-start.78) | collective-permute-done | bytes 917536 | tf_op jit(solution)/shard_map/ppermute | solution.py:22
  390.5 14.0 %collective-permute-done.75 = bf16[2,64,3584]{2,1,0:T(8,128)(2,1)S(1)} collective-permute-done((bf16[2,64,3584]{2,1,0:T(8,128)(2,1)S(1)}, bf16[2,64,3584]{2,1,0:T(8,128)(2,1)S(1)}, u32[]{:S(2)}, u32[]{:S(2)}) %collective-permute-start.75) | collective-permute-done | bytes 917536 | tf_op jit(solution)/shard_map/ppermute | solution.py:22
  407.4 8.7 %fusion.67 = f32[256,2048]{1,0:T(8,128)} fusion(bf16[256,3584]{1,0:T(8,128)(2,1)S(1)} %bitcast.204, bf16[2048,3584]{1,0:T(8,128)(2,1)} %param.9), kind=kOutput, calls=%fused_computation.235 | convolution fusion | flops 3758096384 | bytes 18612224 | tf_op jit(solution)/shard_map/dot_general | solution.py:17
  418.9 11.0 %fusion.66 = f32[256,2048]{1,0:T(8,128)} fusion(bf16[256,3584]{1,0:T(8,128)(2,1)} %bitcast.35, bf16[2048,3584]{1,0:T(8,128)(2,1)} %param.9), kind=kOutput, calls=%fused_computation.234 | convolution fusion | flops 3758096384 | bytes 18612224 | tf_op jit(solution)/shard_map/dot_general | solution.py:17
  429.9 11.2 %fusion.14 = bf16[256,2048]{1,0:T(8,128)(2,1)} fusion(f32[256,2048]{1,0:T(8,128)} %fusion.66, bf16[256,3584]{1,0:T(8,128)(2,1)} %bitcast.206, bf16[2048,3584]{1,0:T(8,128)(2,1)} %param.10), kind=kOutput, calls=%fused_computation.25 | convolution fusion | flops 3759144960 | bytes 19660800 | tf_op jit(solution)/shard_map/dot_general | solution.py:17
  443.0 4.1 collective-permute-start.84
  448.5 16.2 %fusion.15 = bf16[256,2048]{1,0:T(8,128)(2,1)} fusion(f32[256,2048]{1,0:T(8,128)} %fusion.67, bf16[256,3584]{1,0:T(8,128)(2,1)S(1)} %bitcast.201, bf16[2048,3584]{1,0:T(8,128)(2,1)} %param.10), kind=kOutput, calls=%fused_computation.26 | convolution fusion | flops 3759144960 | bytes 19660800 | tf_op jit(solution)/shard_map/dot_general | solution.py:17
  473.1 4.4 collective-permute-start.85
  478.4 4.0 collective-permute-done.85
  482.4 6.8 %collective-permute-start.91 = (bf16[64,2048]{1,0:T(8,128)(2,1)S(1)}, bf16[64,2048]{1,0:T(8,128)(2,1)S(1)}, u32[]{:S(2)}, u32[]{:S(2)}) collective-permute-start(bf16[64,2048]{1,0:T(8,128)(2,1)S(1)} %get-tuple-element.50), channel_id=1, source_target_pairs={{0,2},{2,4},{1,3},{3,5},{8,10},{10,12},{9,11},{11,13},{16,18},{18,... | collective-permute-start | bytes 786440 | tf_op jit(solution)/shard_map/ppermute | solution.py:92
  490.0 4.1 collective-permute-done.91
  494.1 6.3 %collective-permute-start.86 = (bf16[64,2048]{1,0:T(8,128)(2,1)S(1)}, bf16[64,2048]{1,0:T(8,128)(2,1)S(1)}, u32[]{:S(2)}, u32[]{:S(2)}) collective-permute-start(bf16[64,2048]{1,0:T(8,128)(2,1)S(1)} %get-tuple-element.42), channel_id=1, source_target_pairs={{0,2},{2,4},{4,6},{1,3},{3,5},{5,7},{8,10},{10,12},{12,14},{9,11},... | collective-permute-start | bytes 786440 | tf_op jit(solution)/shard_map/ppermute | solution.py:92
  501.9 8.2 %collective-permute-start.92 = (bf16[64,2048]{1,0:T(8,128)(2,1)S(1)}, bf16[64,2048]{1,0:T(8,128)(2,1)S(1)}, u32[]{:S(2)}, u32[]{:S(2)}) collective-permute-start(bf16[64,2048]{1,0:T(8,128)(2,1)S(1)} %get-tuple-element.48), channel_id=1, source_target_pairs={{0,2},{2,4},{4,6},{1,3},{3,5},{5,7},{8,10},{10,12},{12,14},{9,11},... | collective-permute-start | bytes 786440 | tf_op jit(solution)/shard_map/ppermute | solution.py:92
  511.5 15.7 %convolution_add_fusion = f32[1792,2048]{1,0:T(8,128)} fusion(f32[1792,2048]{1,0:T(8,128)} %fusion.19, bf16[512,2048]{1,0:T(8,128)(2,1)} %constant_dynamic-update-slice_fusion, bf16[256,1792]{1,0:T(8,128)(2,1)} %collective-permute-done.80, bf16[256,1792]{1,0:T(8,128)(2,1)S(1)} %copy-done.21), kind=kOutput, calls=%fused_computation | convolution fusion | flops 3765436416 | bytes 33292288 | tf_op jit(solution)/shard_map/dot_general | solution.py:13
  530.0 9.3 %fusion.10 = f32[1024,3584]{1,0:T(8,128)} fusion(bf16[256,3584]{1,0:T(8,128)(2,1)} %collective-permute-done.79, bf16[256,3584]{1,0:T(8,128)(2,1)S(1)} %bitcast.202, bf16[256,1024]{1,0:T(8,128)(2,1)S(1)} %collective-permute-done.43, bf16[256,1024]{1,0:T(8,128)(2,1)S(1)} %get-tuple-element.56), kind=kOutput, calls=%fused_computation.19 | convolution fusion | flops 3767533568 | bytes 19398656 | tf_op jit(solution)/shard_map/dot_general | solution.py:13
  539.4 5.6 fusion.3
  547.0 16.0 %convolution_add_fusion.1 = f32[1024,3584]{1,0:T(8,128)} fusion(f32[1024,3584]{1,0:T(8,128)} %fusion.10, bf16[256,3584]{1,0:T(8,128)(2,1)} %copy-done.38, bf16[256,3584]{1,0:T(8,128)(2,1)} %bitcast.207, bf16[256,1024]{1,0:T(8,128)(2,1)} %copy-done.25, bf16[256,1024]{1,0:T(8,128)(2,1)S(1)} %get-tuple-element.54), kind=kOutput, calls=%fused_computation.1 | convolution fusion | flops 3771203584 | bytes 34078720 | tf_op jit(solution)/shard_map/dot_general | solution.py:13
  563.0 9.8 %convolution_add_fusion.2 = f32[1024,3584]{1,0:T(8,128)} fusion(f32[1024,3584]{1,0:T(8,128)S(1)} %fusion.3, bf16[256,3584]{1,0:T(8,128)(2,1)} %collective-permute-done.36, bf16[256,3584]{1,0:T(8,128)(2,1)} %bitcast.35, bf16[256,1024]{1,0:T(8,128)(2,1)S(1)} %copy-done.26, bf16[256,1024]{1,0:T(8,128)(2,1)S(1)} %get-tuple-element.54), kind=kOutput, calls=%fused_computation.2 | convolution fusion | flops 3771203584 | bytes 34078720 | tf_op jit(solution)/shard_map/dot_general | solution.py:13
  (431 shorter events, 169.8 us)
Async XLA Ops:
  25.0 34.8 %collective-permute-start.40 = (bf16[64,2048]{1,0:T(8,128)(2,1)S(1)}, bf16[64,2048]{1,0:T(8,128)(2,1)S(1)}, u32[]{:S(2)}, u32[]{:S(2)}) collective-permute-start(bf16[64,2048]{1,0:T(8,128)(2,1)S(1)} %collective-permute-done.39), channel_id=1, source_target_pairs={{2,0},{3,1},{10,8},{11,9},{18,16},{19,17},{26,24},{27,25}} | collective-permute-start | bytes 786440 | tf_op jit(solution)/shard_map/ppermute | solution.py:77
  26.3 33.6 %collective-permute-start.42 = (bf16[64,2048]{1,0:T(8,128)(2,1)S(1)}, bf16[64,2048]{1,0:T(8,128)(2,1)S(1)}, u32[]{:S(2)}, u32[]{:S(2)}) collective-permute-start(bf16[64,2048]{1,0:T(8,128)(2,1)S(1)} %collective-permute-done.41), channel_id=1, source_target_pairs={{4,6},{5,7},{12,14},{13,15},{20,22},{21,23},{28,30},{29,31}} | collective-permute-start | bytes 786440 | tf_op jit(solution)/shard_map/ppermute | solution.py:76
  73.3 23.4 %collective-permute-start.7 = (bf16[2,64,3584]{2,1,0:T(8,128)(2,1)S(1)}, bf16[2,64,3584]{2,1,0:T(8,128)(2,1)S(1)}, u32[]{:S(2)}, u32[]{:S(2)}) collective-permute-start(bf16[2,64,3584]{2,1,0:T(8,128)(2,1)S(1)} %dynamic-slice_bitcast_fusion.3), channel_id=1, source_target_pairs={{0,8},{8,0},{16,24},{24,16},{1,9},{9,1},{17,25},{25,17},{2,10},{10... | collective-permute-start | bytes 2752520 | tf_op jit(solution)/shard_map/ppermute | solution.py:22
  75.0 23.6 %collective-permute-start.9 = (bf16[2,64,3584]{2,1,0:T(8,128)(2,1)S(1)}, bf16[2,64,3584]{2,1,0:T(8,128)(2,1)S(1)}, u32[]{:S(2)}, u32[]{:S(2)}) collective-permute-start(bf16[2,64,3584]{2,1,0:T(8,128)(2,1)S(1)} %dynamic-slice_bitcast_fusion.2), channel_id=1, source_target_pairs={{0,16},{8,24},{16,0},{24,8},{1,17},{9,25},{17,1},{25,9},{2,18},{10... | collective-permute-start | bytes 2752520 | tf_op jit(solution)/shard_map/ppermute | solution.py:22
  76.7 39.6 %collective-permute-start.44 = (bf16[2,64,3584]{2,1,0:T(8,128)(2,1)S(1)}, bf16[2,64,3584]{2,1,0:T(8,128)(2,1)S(1)}, u32[]{:S(2)}, u32[]{:S(2)}) collective-permute-start(bf16[2,64,3584]{2,1,0:T(8,128)(2,1)S(1)} %dynamic-slice_bitcast_fusion.1), channel_id=1, source_target_pairs={{0,8},{8,0},{16,24},{24,16},{1,9},{9,1},{17,25},{25,17},{2,10},{10... | collective-permute-start | bytes 2752520 | tf_op jit(solution)/shard_map/ppermute | solution.py:22
  77.4 41.0 %collective-permute-start.46 = (bf16[2,64,3584]{2,1,0:T(8,128)(2,1)S(1)}, bf16[2,64,3584]{2,1,0:T(8,128)(2,1)S(1)}, u32[]{:S(2)}, u32[]{:S(2)}) collective-permute-start(bf16[2,64,3584]{2,1,0:T(8,128)(2,1)S(1)} %dynamic-slice_bitcast_fusion), channel_id=1, source_target_pairs={{0,16},{8,24},{16,0},{24,8},{1,17},{9,25},{17,1},{25,9},{2,18},{10... | collective-permute-start | bytes 2752520 | tf_op jit(solution)/shard_map/ppermute | solution.py:22
  97.0 30.9 %collective-permute-start.8 = (bf16[64,3584]{1,0:T(8,128)(2,1)S(1)}, bf16[64,3584]{1,0:T(8,128)(2,1)S(1)}, u32[]{:S(2)}, u32[]{:S(2)}) collective-permute-start(bf16[64,3584]{1,0:T(8,128)(2,1)S(1)} %fusion.37), channel_id=1, source_target_pairs={{0,16},{8,24},{16,0},{24,8},{1,17},{9,25},{17,1},{25,9},{2,18},{10... | collective-permute-start | bytes 1376264 | tf_op jit(solution)/shard_map/ppermute | solution.py:22
  99.0 28.9 %collective-permute-start.10 = (bf16[64,3584]{1,0:T(8,128)(2,1)S(1)}, bf16[64,3584]{1,0:T(8,128)(2,1)S(1)}, u32[]{:S(2)}, u32[]{:S(2)}) collective-permute-start(bf16[64,3584]{1,0:T(8,128)(2,1)S(1)} %fusion.38), channel_id=1, source_target_pairs={{0,8},{8,0},{16,24},{24,16},{1,9},{9,1},{17,25},{25,17},{2,10},{10... | collective-permute-start | bytes 1376264 | tf_op jit(solution)/shard_map/ppermute | solution.py:22
  116.6 21.1 %collective-permute-start.45 = (bf16[64,3584]{1,0:T(8,128)(2,1)S(1)}, bf16[64,3584]{1,0:T(8,128)(2,1)S(1)}, u32[]{:S(2)}, u32[]{:S(2)}) collective-permute-start(bf16[64,3584]{1,0:T(8,128)(2,1)S(1)} %fusion.39), channel_id=1, source_target_pairs={{0,16},{8,24},{16,0},{24,8},{1,17},{9,25},{17,1},{25,9},{2,18},{10... | collective-permute-start | bytes 1376264 | tf_op jit(solution)/shard_map/ppermute | solution.py:22
  118.7 19.0 %collective-permute-start.47 = (bf16[64,3584]{1,0:T(8,128)(2,1)S(1)}, bf16[64,3584]{1,0:T(8,128)(2,1)S(1)}, u32[]{:S(2)}, u32[]{:S(2)}) collective-permute-start(bf16[64,3584]{1,0:T(8,128)(2,1)S(1)} %fusion.40), channel_id=1, source_target_pairs={{0,8},{8,0},{16,24},{24,16},{1,9},{9,1},{17,25},{25,17},{2,10},{10... | collective-permute-start | bytes 1376264 | tf_op jit(solution)/shard_map/ppermute | solution.py:22
  142.8 13.8 %collective-permute-start.14 = (bf16[2,64,1792]{2,1,0:T(8,128)(2,1)S(1)}, bf16[2,64,1792]{2,1,0:T(8,128)(2,1)S(1)}, u32[]{:S(2)}, u32[]{:S(2)}) collective-permute-start(bf16[2,64,1792]{2,1,0:T(8,128)(2,1)S(1)} %pad_maximum_fusion.30), channel_id=1, source_target_pairs={{0,8},{8,0},{16,24},{24,16},{1,9},{9,1},{17,25},{25,17},{2,10},{10... | collective-permute-start | bytes 1376264 | tf_op jit(solution)/shard_map/ppermute | solution.py:22
  143.3 14.1 %collective-permute-start.12 = (bf16[2,64,1792]{2,1,0:T(8,128)(2,1)S(1)}, bf16[2,64,1792]{2,1,0:T(8,128)(2,1)S(1)}, u32[]{:S(2)}, u32[]{:S(2)}) collective-permute-start(bf16[2,64,1792]{2,1,0:T(8,128)(2,1)S(1)} %pad_maximum_fusion.29), channel_id=1, source_target_pairs={{0,16},{8,24},{16,0},{24,8},{1,17},{9,25},{17,1},{25,9},{2,18},{10... | collective-permute-start | bytes 1376264 | tf_op jit(solution)/shard_map/ppermute | solution.py:22
  147.7 16.1 %collective-permute-start.51 = (bf16[2,64,1792]{2,1,0:T(8,128)(2,1)S(1)}, bf16[2,64,1792]{2,1,0:T(8,128)(2,1)S(1)}, u32[]{:S(2)}, u32[]{:S(2)}) collective-permute-start(bf16[2,64,1792]{2,1,0:T(8,128)(2,1)S(1)} %pad_maximum_fusion.32), channel_id=1, source_target_pairs={{0,8},{8,0},{16,24},{24,16},{1,9},{9,1},{17,25},{25,17},{2,10},{10... | collective-permute-start | bytes 1376264 | tf_op jit(solution)/shard_map/ppermute | solution.py:22
  149.0 15.5 %collective-permute-start.49 = (bf16[2,64,1792]{2,1,0:T(8,128)(2,1)S(1)}, bf16[2,64,1792]{2,1,0:T(8,128)(2,1)S(1)}, u32[]{:S(2)}, u32[]{:S(2)}) collective-permute-start(bf16[2,64,1792]{2,1,0:T(8,128)(2,1)S(1)} %pad_maximum_fusion.31), channel_id=1, source_target_pairs={{0,16},{8,24},{16,0},{24,8},{1,17},{9,25},{17,1},{25,9},{2,18},{10... | collective-permute-start | bytes 1376264 | tf_op jit(solution)/shard_map/ppermute | solution.py:22
  176.5 15.7 %collective-permute-start.53 = (bf16[64,2048]{1,0:T(8,128)(2,1)S(1)}, bf16[64,2048]{1,0:T(8,128)(2,1)S(1)}, u32[]{:S(2)}, u32[]{:S(2)}) collective-permute-start(bf16[64,2048]{1,0:T(8,128)(2,1)S(1)} %get-tuple-element.60), channel_id=1, source_target_pairs={{0,2},{2,4},{1,3},{3,5},{8,10},{10,12},{9,11},{11,13},{16,18},{18,... | collective-permute-start | bytes 786440 | tf_op jit(solution)/shard_map/ppermute | solution.py:92
  182.6 20.3 %collective-permute-start.17 = (bf16[64,2048]{1,0:T(8,128)(2,1)}, bf16[64,2048]{1,0:T(8,128)(2,1)}, u32[]{:S(2)}, u32[]{:S(2)}) collective-permute-start(bf16[64,2048]{1,0:T(8,128)(2,1)} %get-tuple-element.64), channel_id=1, source_target_pairs={{0,2},{2,4},{4,6},{1,3},{3,5},{5,7},{8,10},{10,12},{12,14},{9,11},... | collective-permute-start | bytes 786440 | tf_op jit(solution)/shard_map/ppermute | solution.py:92
  220.5 13.7 %collective-permute-start.62 = (bf16[64,2048]{1,0:T(8,128)(2,1)S(1)}, bf16[64,2048]{1,0:T(8,128)(2,1)S(1)}, u32[]{:S(2)}, u32[]{:S(2)}) collective-permute-start(bf16[64,2048]{1,0:T(8,128)(2,1)S(1)} %get-tuple-element.97), channel_id=1, source_target_pairs={{2,0},{4,2},{6,4},{3,1},{5,3},{7,5},{10,8},{12,10},{14,12},{11,9},... | collective-permute-start | bytes 786440 | tf_op jit(solution)/shard_map/ppermute | solution.py:77
  223.6 23.7 %collective-permute-start.25 = (bf16[64,2048]{1,0:T(8,128)(2,1)S(1)}, bf16[64,2048]{1,0:T(8,128)(2,1)S(1)}, u32[]{:S(2)}, u32[]{:S(2)}) collective-permute-start(bf16[64,2048]{1,0:T(8,128)(2,1)S(1)} %get-tuple-element.13), channel_id=1, source_target_pairs={{2,0},{4,2},{6,4},{3,1},{5,3},{7,5},{10,8},{12,10},{14,12},{11,9},... | collective-permute-start | bytes 786440 | tf_op jit(solution)/shard_map/ppermute | solution.py:77
  225.0 23.6 %collective-permute-start.24 = (bf16[64,2048]{1,0:T(8,128)(2,1)S(1)}, bf16[64,2048]{1,0:T(8,128)(2,1)S(1)}, u32[]{:S(2)}, u32[]{:S(2)}) collective-permute-start(bf16[64,2048]{1,0:T(8,128)(2,1)S(1)} %get-tuple-element.13), channel_id=1, source_target_pairs={{0,2},{2,4},{4,6},{1,3},{3,5},{5,7},{8,10},{10,12},{12,14},{9,11},... | collective-permute-start | bytes 786440 | tf_op jit(solution)/shard_map/ppermute | solution.py:76
  230.3 19.8 %collective-permute-start.61 = (bf16[64,2048]{1,0:T(8,128)(2,1)S(1)}, bf16[64,2048]{1,0:T(8,128)(2,1)S(1)}, u32[]{:S(2)}, u32[]{:S(2)}) collective-permute-start(bf16[64,2048]{1,0:T(8,128)(2,1)S(1)} %get-tuple-element.97), channel_id=1, source_target_pairs={{0,2},{2,4},{4,6},{1,3},{3,5},{5,7},{8,10},{10,12},{12,14},{9,11},... | collective-permute-start | bytes 786440 | tf_op jit(solution)/shard_map/ppermute | solution.py:76
  234.2 18.1 %collective-permute-start.63 = (bf16[64,2048]{1,0:T(8,128)(2,1)S(1)}, bf16[64,2048]{1,0:T(8,128)(2,1)S(1)}, u32[]{:S(2)}, u32[]{:S(2)}) collective-permute-start(bf16[64,2048]{1,0:T(8,128)(2,1)S(1)} %collective-permute-done.62), channel_id=1, source_target_pairs={{2,0},{4,2},{3,1},{5,3},{10,8},{12,10},{11,9},{13,11},{18,16},{20,... | collective-permute-start | bytes 786440 | tf_op jit(solution)/shard_map/ppermute | solution.py:77
  247.3 254.6 %collective-permute-start.80 = (bf16[256,1792]{1,0:T(8,128)(2,1)}, bf16[256,1792]{1,0:T(8,128)(2,1)}, u32[]{:S(2)}, u32[]{:S(2)}) collective-permute-start(bf16[256,1792]{1,0:T(8,128)(2,1)} %get-tuple-element.27), channel_id=1, source_target_pairs={{0,1},{1,0},{2,3},{3,2},{4,5},{5,4},{6,7},{7,6},{8,9},{9,8},{10,11... | collective-permute-start | bytes 2752520 | tf_op jit(solution)/shard_map/ppermute | solution.py:22
  252.3 14.6 %collective-permute-start.64 = (bf16[64,2048]{1,0:T(8,128)(2,1)S(1)}, bf16[64,2048]{1,0:T(8,128)(2,1)S(1)}, u32[]{:S(2)}, u32[]{:S(2)}) collective-permute-start(bf16[64,2048]{1,0:T(8,128)(2,1)S(1)} %collective-permute-done.63), channel_id=1, source_target_pairs={{2,0},{3,1},{10,8},{11,9},{18,16},{19,17},{26,24},{27,25}} | collective-permute-start | bytes 786440 | tf_op jit(solution)/shard_map/ppermute | solution.py:77
  259.0 87.6 %collective-permute-start.82 = (bf16[256,1792]{1,0:T(8,128)(2,1)}, bf16[256,1792]{1,0:T(8,128)(2,1)}, u32[]{:S(2)}, u32[]{:S(2)}) collective-permute-start(bf16[256,1792]{1,0:T(8,128)(2,1)} %get-tuple-element.29), channel_id=1, source_target_pairs={{0,1},{1,0},{2,3},{3,2},{4,5},{5,4},{6,7},{7,6},{8,9},{9,8},{10,11... | collective-permute-start | bytes 2752520 | tf_op jit(solution)/shard_map/ppermute | solution.py:22
  259.0 27.8 %collective-permute-start.27 = (bf16[64,2048]{1,0:T(8,128)(2,1)}, bf16[64,2048]{1,0:T(8,128)(2,1)}, u32[]{:S(2)}, u32[]{:S(2)}) collective-permute-start(bf16[64,2048]{1,0:T(8,128)(2,1)} %collective-permute-done.26), channel_id=1, source_target_pairs={{2,0},{3,1},{10,8},{11,9},{18,16},{19,17},{26,24},{27,25}} | collective-permute-start | bytes 786440 | tf_op jit(solution)/shard_map/ppermute | solution.py:77
  260.3 32.7 %collective-permute-start.29 = (bf16[64,2048]{1,0:T(8,128)(2,1)}, bf16[64,2048]{1,0:T(8,128)(2,1)}, u32[]{:S(2)}, u32[]{:S(2)}) collective-permute-start(bf16[64,2048]{1,0:T(8,128)(2,1)} %collective-permute-done.28), channel_id=1, source_target_pairs={{4,6},{5,7},{12,14},{13,15},{20,22},{21,23},{28,30},{29,31}} | collective-permute-start | bytes 786440 | tf_op jit(solution)/shard_map/ppermute | solution.py:76
  284.5 22.6 %collective-permute-start.67 = (bf16[2,64,1792]{2,1,0:T(8,128)(2,1)}, bf16[2,64,1792]{2,1,0:T(8,128)(2,1)}, u32[]{:S(2)}, u32[]{:S(2)}) collective-permute-start(bf16[2,64,1792]{2,1,0:T(8,128)(2,1)} %dynamic-slice_bitcast_fusion.5), channel_id=1, source_target_pairs={{0,8},{8,0},{16,24},{24,16},{1,9},{9,1},{17,25},{25,17},{2,10},{10... | collective-permute-start | bytes 1376264 | tf_op jit(solution)/shard_map/ppermute | solution.py:22
  286.8 22.1 %collective-permute-start.69 = (bf16[2,64,1792]{2,1,0:T(8,128)(2,1)}, bf16[2,64,1792]{2,1,0:T(8,128)(2,1)}, u32[]{:S(2)}, u32[]{:S(2)}) collective-permute-start(bf16[2,64,1792]{2,1,0:T(8,128)(2,1)} %dynamic-slice_bitcast_fusion.4), channel_id=1, source_target_pairs={{0,16},{8,24},{16,0},{24,8},{1,17},{9,25},{17,1},{25,9},{2,18},{10... | collective-permute-start | bytes 1376264 | tf_op jit(solution)/shard_map/ppermute | solution.py:22
  308.9 48.3 %collective-permute-start.81 = (bf16[256,2048]{1,0:T(8,128)(2,1)S(1)}, bf16[256,2048]{1,0:T(8,128)(2,1)S(1)}, u32[]{:S(2)}, u32[]{:S(2)}) collective-permute-start(bf16[256,2048]{1,0:T(8,128)(2,1)S(1)} %pad_maximum_fusion.10), channel_id=1, source_target_pairs={{0,1},{1,0},{2,3},{3,2},{4,5},{5,4},{6,7},{7,6},{8,9},{9,8},{10,11... | collective-permute-start | bytes 3145736 | tf_op jit(solution)/shard_map/ppermute | solution.py:22
  316.9 28.5 %collective-permute-start.83 = (bf16[256,2048]{1,0:T(8,128)(2,1)S(1)}, bf16[256,2048]{1,0:T(8,128)(2,1)S(1)}, u32[]{:S(2)}, u32[]{:S(2)}) collective-permute-start(bf16[256,2048]{1,0:T(8,128)(2,1)S(1)} %copy-done.39), channel_id=1, source_target_pairs={{0,1},{1,0},{2,3},{3,2},{4,5},{5,4},{6,7},{7,6},{8,9},{9,8},{10,11... | collective-permute-start | bytes 3145736 | tf_op jit(solution)/shard_map/ppermute | solution.py:22
  344.4 15.0 %collective-permute-start.77 = (bf16[64,3584]{1,0:T(8,128)(2,1)S(1)}, bf16[64,3584]{1,0:T(8,128)(2,1)S(1)}, u32[]{:S(2)}, u32[]{:S(2)}) collective-permute-start(bf16[64,3584]{1,0:T(8,128)(2,1)S(1)} %get-tuple-element.24), channel_id=1, source_target_pairs={{0,16},{8,24},{16,0},{24,8},{1,17},{9,25},{17,1},{25,9},{2,18},{10... | collective-permute-start | bytes 1376264 | tf_op jit(solution)/shard_map/ppermute | solution.py:22
  345.4 15.2 %collective-permute-start.71 = (bf16[64,3584]{1,0:T(8,128)(2,1)S(1)}, bf16[64,3584]{1,0:T(8,128)(2,1)S(1)}, u32[]{:S(2)}, u32[]{:S(2)}) collective-permute-start(bf16[64,3584]{1,0:T(8,128)(2,1)S(1)} %get-tuple-element.25), channel_id=1, source_target_pairs={{0,8},{8,0},{16,24},{24,16},{1,9},{9,1},{17,25},{25,17},{2,10},{10... | collective-permute-start | bytes 1376264 | tf_op jit(solution)/shard_map/ppermute | solution.py:22
  346.6 20.4 %collective-permute-start.74 = (bf16[64,3584]{1,0:T(8,128)(2,1)S(1)}, bf16[64,3584]{1,0:T(8,128)(2,1)S(1)}, u32[]{:S(2)}, u32[]{:S(2)}) collective-permute-start(bf16[64,3584]{1,0:T(8,128)(2,1)S(1)} %get-tuple-element.22), channel_id=1, source_target_pairs={{0,16},{8,24},{16,0},{24,8},{1,17},{9,25},{17,1},{25,9},{2,18},{10... | collective-permute-start | bytes 1376264 | tf_op jit(solution)/shard_map/ppermute | solution.py:22
  359.6 30.7 %collective-permute-start.78 = (bf16[2,64,3584]{2,1,0:T(8,128)(2,1)S(1)}, bf16[2,64,3584]{2,1,0:T(8,128)(2,1)S(1)}, u32[]{:S(2)}, u32[]{:S(2)}) collective-permute-start(bf16[2,64,3584]{2,1,0:T(8,128)(2,1)S(1)} %pad_maximum_fusion.24), channel_id=1, source_target_pairs={{0,8},{8,0},{16,24},{24,16},{1,9},{9,1},{17,25},{25,17},{2,10},{10... | collective-permute-start | bytes 2752520 | tf_op jit(solution)/shard_map/ppermute | solution.py:22
  360.8 45.7 %collective-permute-start.72 = (bf16[2,64,3584]{2,1,0:T(8,128)(2,1)S(1)}, bf16[2,64,3584]{2,1,0:T(8,128)(2,1)S(1)}, u32[]{:S(2)}, u32[]{:S(2)}) collective-permute-start(bf16[2,64,3584]{2,1,0:T(8,128)(2,1)S(1)} %pad_maximum_fusion.22), channel_id=1, source_target_pairs={{0,16},{8,24},{16,0},{24,8},{1,17},{9,25},{17,1},{25,9},{2,18},{10... | collective-permute-start | bytes 2752520 | tf_op jit(solution)/shard_map/ppermute | solution.py:22
  367.2 37.3 %collective-permute-start.75 = (bf16[2,64,3584]{2,1,0:T(8,128)(2,1)S(1)}, bf16[2,64,3584]{2,1,0:T(8,128)(2,1)S(1)}, u32[]{:S(2)}, u32[]{:S(2)}) collective-permute-start(bf16[2,64,3584]{2,1,0:T(8,128)(2,1)S(1)} %pad_maximum_fusion.23), channel_id=1, source_target_pairs={{0,8},{8,0},{16,24},{24,16},{1,9},{9,1},{17,25},{25,17},{2,10},{10... | collective-permute-start | bytes 2752520 | tf_op jit(solution)/shard_map/ppermute | solution.py:22
  371.8 44.3 %collective-permute-start.35 = (bf16[2,64,3584]{2,1,0:T(8,128)(2,1)}, bf16[2,64,3584]{2,1,0:T(8,128)(2,1)}, u32[]{:S(2)}, u32[]{:S(2)}) collective-permute-start(bf16[2,64,3584]{2,1,0:T(8,128)(2,1)} %pad_maximum_fusion.18), channel_id=1, source_target_pairs={{0,16},{8,24},{16,0},{24,8},{1,17},{9,25},{17,1},{25,9},{2,18},{10... | collective-permute-start | bytes 2752520 | tf_op jit(solution)/shard_map/ppermute | solution.py:22
  406.8 132.5 %collective-permute-start.73 = (bf16[256,3584]{1,0:T(8,128)(2,1)S(1)}, bf16[256,3584]{1,0:T(8,128)(2,1)}, u32[]{:S(2)}, u32[]{:S(2)}) collective-permute-start(bf16[256,3584]{1,0:T(8,128)(2,1)S(1)} %bitcast.203), channel_id=1, source_target_pairs={{0,1},{1,0},{2,3},{3,2},{4,5},{5,4},{6,7},{7,6},{8,9},{9,8},{10,11... | collective-permute-start | bytes 5505032 | tf_op jit(solution)/shard_map/ppermute | solution.py:22
  406.9 123.1 %collective-permute-start.79 = (bf16[256,3584]{1,0:T(8,128)(2,1)S(1)}, bf16[256,3584]{1,0:T(8,128)(2,1)}, u32[]{:S(2)}, u32[]{:S(2)}) collective-permute-start(bf16[256,3584]{1,0:T(8,128)(2,1)S(1)} %bitcast.200), channel_id=1, source_target_pairs={{0,1},{1,0},{2,3},{3,2},{4,5},{5,4},{6,7},{7,6},{8,9},{9,8},{10,11... | collective-permute-start | bytes 5505032 | tf_op jit(solution)/shard_map/ppermute | solution.py:22
  443.0 22.9 %collective-permute-start.84 = (bf16[64,2048]{1,0:T(8,128)(2,1)}, bf16[64,2048]{1,0:T(8,128)(2,1)S(1)}, u32[]{:S(2)}, u32[]{:S(2)}) collective-permute-start(bf16[64,2048]{1,0:T(8,128)(2,1)} %get-tuple-element.46), channel_id=1, source_target_pairs={{0,2},{1,3},{8,10},{9,11},{16,18},{17,19},{24,26},{25,27}} | collective-permute-start | bytes 786440 | tf_op jit(solution)/shard_map/ppermute | solution.py:92
  447.2 20.1 %collective-permute-start.87 = (bf16[64,2048]{1,0:T(8,128)(2,1)}, bf16[64,2048]{1,0:T(8,128)(2,1)}, u32[]{:S(2)}, u32[]{:S(2)}) collective-permute-start(bf16[64,2048]{1,0:T(8,128)(2,1)} %get-tuple-element.47), channel_id=1, source_target_pairs={{6,4},{7,5},{14,12},{15,13},{22,20},{23,21},{30,28},{31,29}} | collective-permute-start | bytes 786440 | tf_op jit(solution)/shard_map/ppermute | solution.py:93
  494.1 16.0 %collective-permute-start.86 = (bf16[64,2048]{1,0:T(8,128)(2,1)S(1)}, bf16[64,2048]{1,0:T(8,128)(2,1)S(1)}, u32[]{:S(2)}, u32[]{:S(2)}) collective-permute-start(bf16[64,2048]{1,0:T(8,128)(2,1)S(1)} %get-tuple-element.42), channel_id=1, source_target_pairs={{0,2},{2,4},{4,6},{1,3},{3,5},{5,7},{8,10},{10,12},{12,14},{9,11},... | collective-permute-start | bytes 786440 | tf_op jit(solution)/shard_map/ppermute | solution.py:92
  500.5 26.7 %collective-permute-start.89 = (bf16[64,2048]{1,0:T(8,128)(2,1)S(1)}, bf16[64,2048]{1,0:T(8,128)(2,1)S(1)}, u32[]{:S(2)}, u32[]{:S(2)}) collective-permute-start(bf16[64,2048]{1,0:T(8,128)(2,1)S(1)} %get-tuple-element.43), channel_id=1, source_target_pairs={{2,0},{4,2},{6,4},{3,1},{5,3},{7,5},{10,8},{12,10},{14,12},{11,9},... | collective-permute-start | bytes 786440 | tf_op jit(solution)/shard_map/ppermute | solution.py:93
  501.9 25.3 %collective-permute-start.92 = (bf16[64,2048]{1,0:T(8,128)(2,1)S(1)}, bf16[64,2048]{1,0:T(8,128)(2,1)S(1)}, u32[]{:S(2)}, u32[]{:S(2)}) collective-permute-start(bf16[64,2048]{1,0:T(8,128)(2,1)S(1)} %get-tuple-element.48), channel_id=1, source_target_pairs={{0,2},{2,4},{4,6},{1,3},{3,5},{5,7},{8,10},{10,12},{12,14},{9,11},... | collective-permute-start | bytes 786440 | tf_op jit(solution)/shard_map/ppermute | solution.py:92
  510.1 17.6 %collective-permute-start.95 = (bf16[64,2048]{1,0:T(8,128)(2,1)S(1)}, bf16[64,2048]{1,0:T(8,128)(2,1)S(1)}, u32[]{:S(2)}, u32[]{:S(2)}) collective-permute-start(bf16[64,2048]{1,0:T(8,128)(2,1)S(1)} %get-tuple-element.49), channel_id=1, source_target_pairs={{2,0},{4,2},{6,4},{3,1},{5,3},{7,5},{10,8},{12,10},{14,12},{11,9},... | collective-permute-start | bytes 786440 | tf_op jit(solution)/shard_map/ppermute | solution.py:93
  527.2 17.7 %collective-permute-start.6 = (bf16[256,1024]{1,0:T(8,128)(2,1)}, bf16[256,1024]{1,0:T(8,128)(2,1)S(1)}, u32[]{:S(2)}, u32[]{:S(2)}) collective-permute-start(bf16[256,1024]{1,0:T(8,128)(2,1)} %get-tuple-element.55), channel_id=1, source_target_pairs={{0,1},{1,0},{2,3},{3,2},{4,5},{5,4},{6,7},{7,6},{8,9},{9,8},{10,11... | collective-permute-start | bytes 1572872 | tf_op jit(solution)/shard_map/ppermute | solution.py:22
  527.7 17.2 %collective-permute-start.76 = (bf16[256,3584]{1,0:T(8,128)(2,1)S(1)}, bf16[256,3584]{1,0:T(8,128)(2,1)S(1)}, u32[]{:S(2)}, u32[]{:S(2)}) collective-permute-start(bf16[256,3584]{1,0:T(8,128)(2,1)S(1)} %bitcast.208), channel_id=1, source_target_pairs={{0,1},{1,0},{2,3},{3,2},{4,5},{5,4},{6,7},{7,6},{8,9},{9,8},{10,11... | collective-permute-start | bytes 5505032 | tf_op jit(solution)/shard_map/ppermute | solution.py:22
  529.9 33.1 %collective-permute-start.36 = (bf16[256,3584]{1,0:T(8,128)(2,1)}, bf16[256,3584]{1,0:T(8,128)(2,1)}, u32[]{:S(2)}, u32[]{:S(2)}) collective-permute-start(bf16[256,3584]{1,0:T(8,128)(2,1)} %bitcast.35), channel_id=1, source_target_pairs={{0,1},{1,0},{2,3},{3,2},{4,5},{5,4},{6,7},{7,6},{8,9},{9,8},{10,11... | collective-permute-start | bytes 5505032 | tf_op jit(solution)/shard_map/ppermute | solution.py:22
  (127 other events, 1609.8 us)
